TPU v7x, 256 devices: a whole 4x4x8 slice. The times are simulated.
256 devices in a mesh: req: 16 (over y_hi, z), tp: 8 (over x, core), pp: 2 (over y_lo).
Axes of the slice: x: 4, y: 4 (y_hi: 2, y_lo: 2; y = y_hi * 2 + y_lo), z: 8, core: 2. Of those that a mesh axis runs over, the one named last changes fastest.
Arguments:
- prompt_states: bfloat16 [32, 128, 8192], P('tp', 'req', 'pp'), may hold values from -6 to 6
- prompt_lengths: int32 [32], replicated, may hold values from 1 to 128, 2560 in all
- adapter_ids: int32 [32], replicated, may hold values from 0 to 15
- w_query: bfloat16 [8192, 8192], P('pp', 'req'), may hold values from -2 to 2
- w_key: bfloat16 [8192, 1024], P('pp', 'req'), may hold values from -2 to 2
- value_weight: bfloat16 [8192, 1024], P('pp', 'req'), may hold values from -0.0625 to 0.0625
- down_query: bfloat16 [16, 8192, 32], P('req', 'pp'), may hold values from -0.0625 to 0.0625
- up_query: bfloat16 [16, 32, 8192], P(None, None, 'req'), may hold values from -1 to 1
- down_value: bfloat16 [16, 8192, 32], P('req', 'pp'), may hold values from -0.0625 to 0.0625
- value_up_weight: bfloat16 [16, 32, 1024], P(None, None, 'req'), may hold values from -1 to 1
- step_queries: bfloat16 [32, 4, 8192], P(('req', 'pp')), may hold values from -6 to 6
- step_keyvals: bfloat16 [32, 4, 2, 1024], P(('req', 'pp')), may hold values from -6 to 6
Outputs:
- prefill_out: bfloat16 [32, 128, 8192], P('tp', 'pp', 'req')
- decoded: bfloat16 [32, 4, 8192], P(('req', 'pp'))
Inputs may be any that keep to these rules, and one draw needn't show every extreme that they name: `prompt_lengths`: some prompt holds exactly 128 tokens.
All inputs are finite; a program needn't handle non-finite values.
Results may differ from a plain program's by a relative error of at most 0.011.
Values may be sent and summed in bfloat16 or wider, within the bound.
A program may use at most 64 MiB of HBM per device.

v0:
```python
import jax
import jax.numpy as jnp
from jax import lax
from jax.sharding import PartitionSpec as P

HEAD_SIZE = 128
NEG = -1e30


def partner(block, axis, apart):
    count = lax.axis_size(axis)
    route = []
    for low in range(count):
        high = low | 1 << apart
        if high != low and high < count:
            route += [(low, high), (high, low)]
    return lax.ppermute(block, axis, route)


def joined(value, axis, join):
    pieces = jax.tree.map(lambda part: lax.all_gather(part, axis), value)
    head = jax.tree.map(lambda part: part[0], pieces)
    tail = jax.tree.map(lambda part: part[1:], pieces)
    total, _ = lax.scan(lambda total, section: (join(total, section), None), head, tail)
    return total


def combine_partial(first, second):
    top = jnp.maximum(first[0], second[0])
    scale_one = jnp.exp(first[0] - top)
    scale_two = jnp.exp(second[0] - top)
    total = first[1] * scale_one + second[1] * scale_two
    summed = first[2] * scale_one[..., None] + second[2] * scale_two[..., None]
    return (top, total, summed)


def local(
    prompt_states,
    prompt_lengths,
    adapter_ids,
    w_query,
    w_key,
    value_weight,
    down_query,
    up_query,
    down_value,
    value_up_weight,
    step_queries,
    step_keyvals,
):
    single_float = jnp.float32
    bf16 = jnp.bfloat16
    req_count = lax.axis_size("req")
    tp_count = lax.axis_size("tp")
    pp_count = lax.axis_size("pp")
    req_index = lax.axis_index("req")
    tp_index = lax.axis_index("tp")
    pp_index = lax.axis_index("pp")
    prompt_block, pos_block, half_width = prompt_states.shape
    seq_len = pos_block * req_count
    query_cols = w_query.shape[1]
    kv_cols = w_key.shape[1]
    rank = down_query.shape[2]
    scale = HEAD_SIZE ** (-0.5)
    first_prompt = tp_index * prompt_block
    my_lengths = lax.dynamic_slice_in_dim(prompt_lengths, first_prompt, prompt_block)
    my_adapters = lax.dynamic_slice_in_dim(adapter_ids, first_prompt, prompt_block)
    table_query, table_value = (
        lax.all_gather(down_query, "req", axis=0, tiled=True),
        lax.all_gather(down_value, "req", axis=0, tiled=True),
    )
    rank_query = jnp.take(table_query, my_adapters, axis=0)
    rank_value = jnp.take(table_value, my_adapters, axis=0)
    piece = lax.all_gather(prompt_states, "req", axis=1, tiled=True)
    count = piece.shape[1]
    flat = piece.reshape(prompt_block * count, half_width)
    base_query = jnp.dot(flat, w_query, preferred_element_type=single_float)
    base_key = jnp.dot(flat, w_key, preferred_element_type=single_float)
    base_value = jnp.dot(flat, value_weight, preferred_element_type=single_float)
    dense = jnp.concatenate([base_query, base_key, base_value], axis=1).reshape(
        prompt_block, count, -1
    )
    low_query = jnp.einsum("pnd,pdr->pnr", piece, rank_query, preferred_element_type=single_float)
    low_value = jnp.einsum("pnd,pdr->pnr", piece, rank_value, preferred_element_type=single_float)
    packed = jnp.concatenate([dense, low_query, low_value], axis=2)
    query_part = packed[:, :, :query_cols]
    kv_part = packed[:, :, query_cols : query_cols + 2 * kv_cols]
    low_part = packed[:, :, query_cols + 2 * kv_cols :]
    query_sum, kv_sum, low_sum = lax.psum((query_part, kv_part, low_part), "pp")
    query_len = query_sum.shape[1]
    low_query = low_sum[:, :, :rank].astype(bf16)
    low_value = low_sum[:, :, rank:].astype(bf16)
    up_query_rows = jnp.take(up_query, my_adapters, axis=0)
    up_value_rows = jnp.take(value_up_weight, my_adapters, axis=0)
    query_rows = (
        query_sum
        + jnp.einsum("pnr,prc->pnc", low_query, up_query_rows, preferred_element_type=single_float)
    ).astype(bf16)
    keys_own = kv_sum[:, :, :kv_cols].astype(bf16)
    values_own = (
        kv_sum[:, :, kv_cols:]
        + jnp.einsum("pnr,prc->pnc", low_value, up_value_rows, preferred_element_type=single_float)
    ).astype(bf16)
    keys_all = keys_own
    values_all = values_own
    other_keys, other_values = partner((keys_all, values_all), "req", 0)
    upper = req_index // 2**0 % 2 == 1
    keys_all = jnp.where(
        upper,
        jnp.concatenate([other_keys, keys_all], axis=2),
        jnp.concatenate([keys_all, other_keys], axis=2),
    )
    values_all = jnp.where(
        upper,
        jnp.concatenate([other_values, values_all], axis=2),
        jnp.concatenate([values_all, other_values], axis=2),
    )
    local_kv = keys_all.shape[2] // HEAD_SIZE
    local_query = query_cols // HEAD_SIZE
    per_kv = local_query // local_kv
    query_heads = query_rows.reshape(prompt_block, query_len, local_kv, per_kv, HEAD_SIZE)
    key_heads = keys_all.reshape(prompt_block, seq_len, local_kv, HEAD_SIZE)
    value_heads = values_all.reshape(prompt_block, seq_len, local_kv, HEAD_SIZE)
    scores = (
        jnp.einsum("pikgd,pjkd->pkgij", query_heads, key_heads, preferred_element_type=single_float)
        * scale
    )
    rows = jnp.arange(query_len, dtype=jnp.int32)
    cols = jnp.arange(seq_len, dtype=jnp.int32)
    allowed = (cols[None, None, :] <= rows[None, :, None]) & (
        cols[None, None, :] < my_lengths[:, None, None]
    )
    scores = jnp.where(allowed[:, None, None], scores, NEG)
    top = jnp.max(scores, axis=-1, keepdims=True)
    raised = jnp.exp(scores - top)
    weights = (raised / jnp.sum(raised, axis=-1, keepdims=True)).astype(bf16)
    mixed = jnp.einsum(
        "pkgij,pjkd->pikgd", weights, value_heads, preferred_element_type=single_float
    )
    live_rows = rows[None, :] < my_lengths[:, None]
    mixed = jnp.where(live_rows[:, :, None, None, None], mixed, 0.0)
    mixed = mixed.reshape(prompt_block, query_len, query_cols).astype(bf16)
    share = seq_len // pp_count
    prefill_out = lax.dynamic_slice_in_dim(mixed, pp_index * share, share, 1)
    pos_share = seq_len // (tp_count * pp_count)
    stacked = jnp.stack([keys_own, values_own], axis=2)
    stacked = stacked.reshape(prompt_block, tp_count, pp_count, pos_share, 2, kv_cols)
    own_slots = lax.dynamic_index_in_dim(stacked, pp_index, 2, keepdims=False)
    cache = lax.all_to_all(
        lax.all_to_all(own_slots, "tp", split_axis=1, concat_axis=0, tiled=True),
        ("req", "pp"),
        split_axis=0,
        concat_axis=1,
        tiled=True,
    )
    req_dev = step_queries.shape[0]
    steps = step_queries.shape[1]
    cache = cache.reshape(req_dev, req_count, pp_count, pos_share, 2, kv_cols)
    block_len = pp_count * pos_share
    cache = cache.transpose(0, 4, 2, 3, 1, 5).reshape(req_dev, 2, block_len, req_count * kv_cols)
    first_request = (req_index * pp_count + pp_index) * req_dev
    request_lengths = lax.dynamic_slice_in_dim(prompt_lengths, first_request, req_dev)
    heads_kv = cache.shape[3] // HEAD_SIZE
    head_group = step_queries.shape[2] // cache.shape[3]
    step_heads = step_queries.reshape(req_dev, steps, heads_kv, head_group, HEAD_SIZE)
    cached_keys = cache[:, 0].reshape(req_dev, block_len, heads_kv, HEAD_SIZE)
    cached_values = (
        cache[:, 1].reshape(req_dev, block_len, heads_kv, HEAD_SIZE).astype(single_float)
    )
    positions = tp_index * block_len + jnp.arange(block_len, dtype=jnp.int32)
    live = (positions[None, :] < request_lengths[:, None])[:, None, None, None, :]
    old_scores = (
        jnp.einsum(
            "nskgd,nckd->nkgsc", step_heads, cached_keys, preferred_element_type=single_float
        )
        * scale
    )
    old_scores = jnp.where(live, old_scores, NEG)
    old_top = jnp.max(old_scores, axis=-1)
    old_raised = jnp.where(live, jnp.exp(old_scores - old_top[..., None]), 0.0)
    old_total = jnp.sum(old_raised, axis=-1)
    old_summed = jnp.einsum(
        "nkgsc,nckd->nkgsd", old_raised, cached_values, precision=lax.Precision.HIGHEST
    )
    top_all, total_all, summed_all = joined((old_top, old_total, old_summed), "tp", combine_partial)
    new_keys = step_keyvals[:, :, 0].reshape(req_dev, steps, heads_kv, HEAD_SIZE)
    new_values = (
        step_keyvals[:, :, 1].astype(single_float).reshape(req_dev, steps, heads_kv, HEAD_SIZE)
    )
    new_scores = (
        jnp.einsum("nskgd,ntkd->nkgst", step_heads, new_keys, preferred_element_type=single_float)
        * scale
    )
    causal = jnp.arange(steps)[None, :] <= jnp.arange(steps)[:, None]
    new_scores = jnp.where(causal, new_scores, NEG)
    final_top = jnp.maximum(top_all, jnp.max(new_scores, axis=-1))
    old_scale = jnp.exp(top_all - final_top)
    new_raised = jnp.where(causal, jnp.exp(new_scores - final_top[..., None]), 0.0)
    total_final = total_all * old_scale + jnp.sum(new_raised, axis=-1)
    summed_final = summed_all * old_scale[..., None] + jnp.einsum(
        "nkgst,ntkd->nkgsd", new_raised, new_values, precision=lax.Precision.HIGHEST
    )
    decoded = (
        (summed_final / total_final[..., None])
        .transpose(0, 3, 1, 2, 4)
        .reshape(req_dev, steps, step_queries.shape[2])
        .astype(bf16)
    )
    return (prefill_out, decoded)


def solution(mesh):
    in_specs = (
        P("tp", "req", "pp"),
        P(),
        P(),
        P("pp", "req"),
        P("pp", "req"),
        P("pp", "req"),
        P("req", "pp", None),
        P(None, None, "req"),
        P("req", "pp", None),
        P(None, None, "req"),
        P(("req", "pp"), None, None),
        P(("req", "pp"), None, None, None),
    )
    out_specs = (P("tp", "pp", "req"), P(("req", "pp"), None, None))
    return jax.shard_map(local, mesh=mesh, in_specs=in_specs, out_specs=out_specs, check_vma=False)
```

profile of v0, /device:TPU:1, one launch (start us, length us, event | category | flops | bytes accessed | tf_op | source)
XLA Modules:
  0.0 455.7 jit_solution(4399709015090550969)
XLA Ops:
  7.2 0.7 all-gather.8.cloned.1.call-update
  8.0 0.7 all-gather.12.cloned.1.call-update
  8.7 0.7 all-gather.10.cloned.1.call-update
  9.5 0.7 dynamic_slice.27
  10.2 0.7 compare_and_fusion
  10.9 1.5 gather_fusion
  12.4 98.9 %all-gather.8.cloned.1.call-done = bf16[4,128,4096]{2,1,0:T(8,128)(2,1)} async-done(((bf16[4,8,4096]{2,1,0:T(8,128)(2,1)}), bf16[4,128,4096]{2,1,0:T(8,128)(2,1)}) %all-gather.8.cloned.1.call-update) | async-done | bytes 4194320 | tf_op jit(solution)/shard_map/all_gather | solution.py:74
  111.3 3.8 fusion.90
  115.2 1.4 fusion.91
  116.6 2.4 fusion.89
  119.1 0.5 reshape.253
  119.6 1.3 copy.96
  121.0 0.7 copy.95
  121.8 88.6 %all-gather.12.cloned.1.call-done = bf16[16,4096,32]{1,2,0:T(8,128)(2,1)} async-done(((bf16[1,4096,32]{1,2,0:T(8,128)(2,1)}), bf16[16,4096,32]{1,2,0:T(8,128)(2,1)}) %all-gather.12.cloned.1.call-update) | async-done | bytes 4194320 | tf_op jit(solution)/shard_map/all_gather | solution.py:70
  210.4 2.8 gather_fusion.3
  213.2 96.3 %all-gather.10.cloned.1.call-done = bf16[16,4096,32]{1,2,0:T(8,128)(2,1)} async-done(((bf16[1,4096,32]{1,2,0:T(8,128)(2,1)}), bf16[16,4096,32]{1,2,0:T(8,128)(2,1)}) %all-gather.10.cloned.1.call-update) | async-done | bytes 4194320 | tf_op jit(solution)/shard_map/all_gather | solution.py:69
  309.6 2.8 gather_fusion.2
  312.4 3.8 convolution_bitcast_fusion.2
  316.3 1.5 convolution_bitcast_fusion.3
  317.8 6.8 %all-reduce.5 = bf16[4,128,64]{1,2,0:T(8,128)(2,1)S(1)} all-reduce(f32[4,128,64]{1,2,0:T(8,128)S(1)} %pad_maximum_fusion.1), channel_id=1, replica_groups=mesh['req'=16,'tp'=8,'pp'=2] {'pp'}, use_global_device_ids=true, to_apply=%region_1.3 | all-reduce | flops 32768 | bytes 196608 | tf_op jit(solution)/shard_map/psum | solution.py:89
  324.6 46.1 %all-reduce.4.cloned.1.call-done = (f32[4,128,512]{2,1,0:T(8,128)}, f32[4,128,128]{1,2,0:T(8,128)}) async-done(((f32[4,128,512]{2,1,0:T(8,128)}, f32[4,128,128]{1,2,0:T(8,128)}), (f32[4,128,512]{2,1,0:T(8,128)}, f32[4,128,128]{1,2,0:T(8,128)})) %all-reduce.4.cloned.1.call-update) | async-done | bytes 1310736 | tf_op jit(solution)/shard_map/psum | solution.py:89
  370.7 1.0 slice.108
  371.7 1.2 fusion.16
  373.2 0.8 reshape.325
  374.0 4.9 %all-to-all-start = ((bf16[8,2,2048]{2,1,0:T(2,128)(2,1)}), bf16[8,2,2048]{2,1,0:T(2,128)(2,1)S(1)}, u32[]{:S(2)}, u32[]{:S(2)}) async-start(bf16[8,2,2048]{2,1,0:T(2,128)(2,1)} %reshape.325), calls=%async_computation | async-start | bytes 131072 | tf_op jit(solution)/shard_map/all_to_all | solution.py:150
  378.9 0.1 broadcast_and_fusion
  379.1 0.6 dynamic_slice.30
  379.7 4.1 all-to-all-done
  383.8 0.1 reshape.326
  383.9 0.8 reshape.327
  384.7 9.3 %all-to-all-start.1 = ((bf16[32,2,512]{2,1,0:T(2,128)(2,1)}), bf16[32,2,512]{2,1,0:T(2,128)(2,1)S(1)}, u32[]{:S(2)}, u32[]{:S(2)}) async-start(bf16[32,2,512]{2,1,0:T(2,128)(2,1)} %reshape.327), calls=%async_computation.1 | async-start | bytes 131072 | tf_op jit(solution)/shard_map/all_to_all | solution.py:149
  394.0 0.7 add_compare_fusion
  394.8 8.5 %all-to-all-done.1 = bf16[32,2,512]{2,1,0:T(2,128)(2,1)S(1)} async-done(((bf16[32,2,512]{2,1,0:T(2,128)(2,1)}), bf16[32,2,512]{2,1,0:T(2,128)(2,1)S(1)}, u32[]{:S(2)}, u32[]{:S(2)}) %all-to-all-start.1) | async-done | bytes 65568 | tf_op jit(solution)/shard_map/all_to_all | solution.py:149
  403.3 0.1 reshape.328
  403.5 0.1 reshape.257
  403.7 0.2 fusion.87
  403.9 0.9 fusion.48
  404.9 0.6 gather_fusion.1
  405.5 0.4 fusion.88
  405.9 0.4 collective-permute-start.1
  406.4 1.1 collective-permute-start
  407.5 0.4 fusion.11
  407.8 1.3 collective-permute-done.1
  409.1 0.4 fusion.86
  409.5 0.2 fusion.26
  409.7 0.2 collective-permute-done
  409.8 0.4 fusion.9
  410.2 0.2 constant_dynamic-slice_fusion.1
  410.4 0.9 copy.97
  411.3 0.2 fusion.54
  411.5 15.9 %all-gather.1 = f32[64,8,4]{1,2,0:T(4,128)S(1)} all-gather(f32[8,8,4]{1,2,0:T(4,128)S(1)} %fusion.54), channel_id=3, replica_groups=mesh['req'=16,'tp'=8,'pp'=2] {'tp'}, dimensions={0}, use_global_device_ids=true | all-gather | bytes 9216 | tf_op jit(solution)/shard_map/all_gather | solution.py:21
  427.5 12.8 %all-gather = f32[64,8,4]{1,2,0:T(4,128)S(1)} all-gather(f32[8,8,4]{1,2,0:T(4,128)S(1)} %get-tuple-element.96), channel_id=2, replica_groups=mesh['req'=16,'tp'=8,'pp'=2] {'tp'}, dimensions={0}, use_global_device_ids=true | all-gather | bytes 9216 | tf_op jit(solution)/shard_map/all_gather | solution.py:21
  440.3 0.9 slice_bitcast_fusion
  441.3 1.2 slice.94
  442.5 5.4 %while.14 = (s32[]{:T(128)}, f32[1,8,8,4]{2,3,1,0:T(4,128)S(1)}, f32[1,8,8,4]{2,3,1,0:T(4,128)S(1)}, f32[1,8,8,4,128]{4,3,2,1,0:T(4,128)S(1)}, f32[7,1,8,8,4]{3,...) while((s32[]{:T(128)}, f32[1,8,8,4]{2,3,1,0:T(4,128)S(1)}, ...), condition=%wide.region_8.10_spmd, body=%wide.region_7.9_spmd.sunk | while | flops 100098 | bytes 674913 | solution.py:24
  442.9 0.4 fusion.106
  443.6 0.4 fusion.106
  444.4 0.4 fusion.106
  445.2 0.4 fusion.106
  445.9 0.4 fusion.106
  446.7 0.4 fusion.106
  447.5 0.4 fusion.106
  448.1 0.4 fusion.19
  448.5 0.7 convert_element_type.48
  (95 shorter events, 3.5 us)
Async XLA Ops:
  7.2 397.8 %copy-start = (bf16[16,32,512]{2,1,0:T(8,128)(2,1)S(1)}, bf16[16,32,512]{2,1,0:T(8,128)(2,1)}, u32[]{:S(2)}) copy-start(bf16[16,32,512]{2,1,0:T(8,128)(2,1)} %param.23) | copy-start | bytes 1572868
  7.2 108.0 %copy-start.4 = (bf16[4096,64]{0,1:T(8,128)(2,1)S(1)}, bf16[4096,64]{0,1:T(8,128)(2,1)}, u32[]{:S(2)}) copy-start(bf16[4096,64]{0,1:T(8,128)(2,1)} %param.21) | copy-start | bytes 1572868
  7.2 104.1 %all-gather.8.cloned.1.call-start = ((), (), s32[]{:S(2)}) async-start(), calls=%async_computation.2 | async-start | bytes 4456448 | tf_op jit(solution)/shard_map/all_gather | solution.py:74
  7.9 202.5 %all-gather.12.cloned.1.call-start = ((), (), s32[]{:S(2)}) async-start(), calls=%async_computation.4 | async-start | bytes 4456448 | tf_op jit(solution)/shard_map/all_gather | solution.py:70
  8.7 300.9 %all-gather.10.cloned.1.call-start = ((), (), s32[]{:S(2)}) async-start(), calls=%async_computation.3 | async-start | bytes 4456448 | tf_op jit(solution)/shard_map/all_gather | solution.py:69
  9.4 361.3 %all-reduce.4.cloned.1.call-start = ((), (), s32[]{:S(2)}) async-start(), calls=%async_computation.6 | async-start | bytes 2621440 | tf_op jit(solution)/shard_map/psum | solution.py:89
  111.3 3.9 copy-start.1
  111.3 5.3 %copy-start.6 = (bf16[4096,512]{1,0:T(8,128)(2,1)S(1)}, bf16[4096,512]{1,0:T(8,128)(2,1)}, u32[]{:S(2)}) copy-start(bf16[4096,512]{1,0:T(8,128)(2,1)} %param.19) | copy-start | bytes 12582916
  312.4 3.9 copy-start.2
  316.2 62.9 %copy-start.8 = (s32[32]{0:T(128)S(1)}, s32[32]{0:T(128)}, u32[]{:S(2)}) copy-start(s32[32]{0:T(128)} %param.17) | copy-start | bytes 388
  316.2 78.5 %copy-start.5 = (bf16[1,4,2,1024]{3,2,1,0:T(2,128)(2,1)S(1)}, bf16[1,4,2,1024]{3,2,1,0:T(2,128)(2,1)}, u32[]{:S(2)}) copy-start(bf16[1,4,2,1024]{3,2,1,0:T(2,128)(2,1)} %param.27) | copy-start | bytes 49156
  316.3 87.4 %copy-start.7 = (bf16[1,4,8192]{2,1,0:T(4,128)(2,1)S(1)}, bf16[1,4,8192]{2,1,0:T(4,128)(2,1)}, u32[]{:S(2)}) copy-start(bf16[1,4,8192]{2,1,0:T(4,128)(2,1)} %param.26) | copy-start | bytes 196612
  370.7 36.8 %copy-start.3 = (f32[4,128,512]{2,1,0:T(8,128)S(1)}, f32[4,128,512]{2,1,0:T(8,128)}, u32[]{:S(2)}) copy-start(f32[4,128,512]{2,1,0:T(8,128)} %get-tuple-element.82) | copy-start | bytes 3145732
  374.0 9.8 %all-to-all-start = ((bf16[8,2,2048]{2,1,0:T(2,128)(2,1)}), bf16[8,2,2048]{2,1,0:T(2,128)(2,1)S(1)}, u32[]{:S(2)}, u32[]{:S(2)}) async-start(bf16[8,2,2048]{2,1,0:T(2,128)(2,1)} %reshape.325), calls=%async_computation | async-start | bytes 131072 | tf_op jit(solution)/shard_map/all_to_all | solution.py:150
  384.7 18.6 %all-to-all-start.1 = ((bf16[32,2,512]{2,1,0:T(2,128)(2,1)}), bf16[32,2,512]{2,1,0:T(2,128)(2,1)S(1)}, u32[]{:S(2)}, u32[]{:S(2)}) async-start(bf16[32,2,512]{2,1,0:T(2,128)(2,1)} %reshape.327), calls=%async_computation.1 | async-start | bytes 131072 | tf_op jit(solution)/shard_map/all_to_all | solution.py:149
  394.0 46.3 %all-gather.14.cloned.1.call-start = ((), (), s32[]{:S(2)}) async-start(), calls=%async_computation.5 | async-start | bytes 1179648 | tf_op jit(solution)/shard_map/all_gather | solution.py:21
  405.9 3.2 collective-permute-start.1
  406.4 3.5 collective-permute-start
Sparse Core Ops, SparseCore 0:
  10.6 100.6 all-gather.7
  113.9 96.4 all-gather.11
  213.0 96.4 all-gather.9
  312.6 58.0 all-reduce.3
  405.0 20.3 all-gather.13
where the time goes:
time: 456 us
  waiting for transfers between devices  346 us (76%)
  blocking collectives  35.5 us (8%)
  local copies, waits for them, and re-layouts  20.8 us (5%)
  matrix products  17.2 us (4%)
  starting transfers between devices  15.9 us (3%)
  between operations  14.2 us (3%)
  other arithmetic  5.67 us (1%)
    all_gather x1, waiting for transfers between devices, local(): piece = lax.all_gather(prompt_states, 'req', axis=1, tiled=True)  98.9 us
    all_gather x1, waiting for transfers between devices, local(): lax.all_gather(down_query, 'req', axis=0, tiled=True)  96.3 us
    all_gather x1, waiting for transfers between devices, local(): lax.all_gather(down_value, 'req', axis=0, tiled=True)  88.6 us
    psum x1, waiting for transfers between devices, local(): query_sum, kv_sum, low_sum = lax.psum((query_part, kv_part, low_part), 'pp')  46.1 us
    all_gather x2, blocking collectives, joined(): pieces = jax.tree.map(lambda part: lax.all_gather(part, axis), value)  28.7 us
    all_to_all x1, starting transfers between devices, local(): lax.all_to_all(lax.all_to_all(own_slots, 'tp', split_axis=1, concat_axis=...  9.28 us
  transfers between devices with their start and end apart: 9, of which 8 were waited for; matrix products, arithmetic and copies ran while one was open for 6% of the time, Pallas kernels for 0%

commit v1 on v0

--- a/solution.py
+++ b/solution.py
@@ -71,7 +71,9 @@
     )
     rank_query = jnp.take(table_query, my_adapters, axis=0)
     rank_value = jnp.take(table_value, my_adapters, axis=0)
-    piece = lax.all_gather(prompt_states, "req", axis=1, tiled=True)
+    piece = jnp.concatenate(
+        lax.all_to_all(jnp.stack([prompt_states] * lax.axis_size("req")), "req", 0, 0), axis=1
+    )
     count = piece.shape[1]
     flat = piece.reshape(prompt_block * count, half_width)
     base_query = jnp.dot(flat, w_query, preferred_element_type=single_float)

time: 456 us -> 371 us (0.81)
  waiting for transfers between devices: 346 us -> 241 us
  starting transfers between devices: 15.9 us -> 29.7 us
  local copies, waits for them, and re-layouts: 20.8 us -> 26.2 us
    all_to_all x0 -> x1, waiting for transfers between devices: none -> 109 us  [local(): lax.all_to_all(jnp.stack([prompt_states] * lax.axis_size('req')), 'req',...]
    all_gather x1 -> x0, waiting for transfers between devices: 98.9 us -> none  [local(): piece = lax.all_gather(prompt_states, 'req', axis=1, tiled=True)]
    all_gather x1, waiting for transfers between devices: 96.3 us -> 20 us  [local(): lax.all_gather(down_query, 'req', axis=0, tiled=True)]
    psum x1, waiting for transfers between devices: 46.1 us -> 0.03 us  [local(): query_sum, kv_sum, low_sum = lax.psum((query_part, kv_part, low_part), 'pp')]
    all_to_all x0 -> x1, starting transfers between devices: none -> 11.9 us  [local(): lax.all_to_all(jnp.stack([prompt_states] * lax.axis_size('req')), 'req',...]
    all_gather x1, waiting for transfers between devices: 88.6 us -> 96.2 us  [local(): lax.all_gather(down_value, 'req', axis=0, tiled=True)]
    all_to_all x1, starting transfers between devices: 4.92 us -> 10.2 us  [local(): lax.all_to_all(own_slots, 'tp', split_axis=1, concat_axis=0, tiled=True)]
  transfers between devices with their start and end apart: 9 -> 9, of which waited for: 8 -> 7; matrix products, arithmetic and copies ran while one was open for 6% -> 9% of each run, Pallas kernels for 0% -> 0%
where the time goes in v1:
time: 371 us; the launch traced here: 370 us
  waiting for transfers between devices  241 us (65%)
  blocking collectives  35.5 us (10%)
  starting transfers between devices  29.7 us (8%)
  local copies, waits for them, and re-layouts  26.2 us (7%)
  matrix products  16.8 us (5%)
  between operations  16 us (4%)
  other arithmetic  5.02 us (1%)
    all_to_all x1, waiting for transfers between devices, local(): lax.all_to_all(jnp.stack([prompt_states] * lax.axis_size('req')), 'req',...  109 us
    all_gather x1, waiting for transfers between devices, local(): lax.all_gather(down_value, 'req', axis=0, tiled=True)  96.2 us
    all_gather x2, blocking collectives, joined(): pieces = jax.tree.map(lambda part: lax.all_gather(part, axis), value)  28.7 us
    all_gather x1, waiting for transfers between devices, local(): lax.all_gather(down_query, 'req', axis=0, tiled=True)  20 us
    all_to_all x1, starting transfers between devices, local(): lax.all_to_all(jnp.stack([prompt_states] * lax.axis_size('req')), 'req',...  11.9 us
    all_to_all x1, starting transfers between devices, local(): lax.all_to_all(own_slots, 'tp', split_axis=1, concat_axis=0, tiled=True)  10.2 us
    all_to_all x1, waiting for transfers between devices, local(): lax.all_to_all(lax.all_to_all(own_slots, 'tp', split_axis=1, concat_axis=...  8.47 us
  transfers between devices with their start and end apart: 9, of which 7 were waited for; matrix products, arithmetic and copies ran while one was open for 9% of the time, Pallas kernels for 0%

profile of v1, /device:TPU:1, one launch (start us, length us, event | category | flops | bytes accessed | tf_op | source)
XLA Modules:
  0.0 370.5 jit_solution(15408314082120138545)
XLA Ops:
  8.1 0.7 all-gather.7.cloned.1.call-update
  8.7 3.4 stack.8
  12.1 11.9 %all-to-all-start = ((bf16[16,4,8,4096]{3,2,1,0:T(8,128)(2,1)}), bf16[16,4,8,4096]{3,2,1,0:T(8,128)(2,1)}, u32[]{:S(2)}, u32[]{:S(2)}) async-start(bf16[16,4,8,4096]{3,2,1,0:T(8,128)(2,1)} %stack.8), calls=%async_computation | async-start | bytes 8388608 | tf_op jit(solution)/shard_map/all_to_all | solution.py:75
  24.1 0.7 all-gather.9.cloned.1.call-update
  25.0 109.3 %all-to-all-done = bf16[16,4,8,4096]{3,2,1,0:T(8,128)(2,1)} async-done(((bf16[16,4,8,4096]{3,2,1,0:T(8,128)(2,1)}), bf16[16,4,8,4096]{3,2,1,0:T(8,128)(2,1)}, u32[]{:S(2)}, u32[]{:S(2)}) %all-to-all-start) | async-done | bytes 4194336 | tf_op jit(solution)/shard_map/all_to_all | solution.py:75
  134.3 2.7 copy.78
  137.0 1.4 fusion.102
  138.4 1.4 fusion.103
  139.8 2.4 fusion.101
  142.3 0.5 reshape.258
  142.9 1.3 copy.123
  144.2 0.7 copy.122
  145.1 1.5 gather_fusion
  146.6 20.0 %all-gather.7.cloned.1.call-done = bf16[16,4096,32]{1,2,0:T(8,128)(2,1)} async-done(((bf16[1,4096,32]{1,2,0:T(8,128)(2,1)}), bf16[16,4096,32]{1,2,0:T(8,128)(2,1)}) %all-gather.7.cloned.1.call-update) | async-done | bytes 4194320 | tf_op jit(solution)/shard_map/all_gather | solution.py:69
  166.6 2.8 gather_fusion.2
  169.5 96.2 %all-gather.9.cloned.1.call-done = bf16[16,4096,32]{1,2,0:T(8,128)(2,1)} async-done(((bf16[1,4096,32]{1,2,0:T(8,128)(2,1)}), bf16[16,4096,32]{1,2,0:T(8,128)(2,1)}) %all-gather.9.cloned.1.call-update) | async-done | bytes 4194320 | tf_op jit(solution)/shard_map/all_gather | solution.py:70
  265.7 2.8 gather_fusion.3
  268.5 3.7 fusion.24
  272.2 3.7 %fusion.27 = f32[4,128,32]{1,2,0:T(8,128)S(1)} fusion(bf16[4,4096,32]{1,2,0:T(8,128)(2,1)S(1)} %gather_fusion.3, pred[4]{0:T(512)(128)(4,1)S(1)} %get-tuple-element.93, bf16[16,4,8,4096]{3,2,1,0:T(8,128)(2,1)} %all-to-all-done), kind=kOutput, calls=%fused_computation.42 | convolution fusion | flops 134742016 | bytes 5308420 | tf_op jit(solution)/shard_map/pnd,pdr->pnr/dot_general | solution.py:86
  276.0 6.8 %all-reduce.5 = bf16[4,128,64]{1,2,0:T(8,128)(2,1)S(1)} all-reduce(f32[4,128,64]{1,2,0:T(8,128)S(1)} %pad_maximum_fusion.1), channel_id=1, replica_groups=mesh['req'=16,'tp'=8,'pp'=2] {'pp'}, use_global_device_ids=true, to_apply=%region_1.3 | all-reduce | flops 32768 | bytes 196608 | tf_op jit(solution)/shard_map/psum | solution.py:91
  282.8 1.0 slice.108
  283.8 1.2 fusion.20
  285.0 0.1 copy.86
  285.3 0.8 reshape.331
  286.1 10.2 %all-to-all-start.1 = ((bf16[8,2,2048]{2,1,0:T(2,128)(2,1)}), bf16[8,2,2048]{2,1,0:T(2,128)(2,1)S(1)}, u32[]{:S(2)}, u32[]{:S(2)}) async-start(bf16[8,2,2048]{2,1,0:T(2,128)(2,1)} %reshape.331), calls=%async_computation.1 | async-start | bytes 131072 | tf_op jit(solution)/shard_map/all_to_all | solution.py:152
  296.3 0.1 broadcast_and_fusion
  296.5 0.6 dynamic_slice.30
  297.1 4.1 %all-to-all-done.1 = bf16[8,2,2048]{2,1,0:T(2,128)(2,1)S(1)} async-done(((bf16[8,2,2048]{2,1,0:T(2,128)(2,1)}), bf16[8,2,2048]{2,1,0:T(2,128)(2,1)S(1)}, u32[]{:S(2)}, u32[]{:S(2)}) %all-to-all-start.1) | async-done | bytes 65568 | tf_op jit(solution)/shard_map/all_to_all | solution.py:152
  301.2 0.1 reshape.332
  301.3 0.8 reshape.333
  302.1 5.6 %all-to-all-start.2 = ((bf16[32,2,512]{2,1,0:T(2,128)(2,1)}), bf16[32,2,512]{2,1,0:T(2,128)(2,1)S(1)}, u32[]{:S(2)}, u32[]{:S(2)}) async-start(bf16[32,2,512]{2,1,0:T(2,128)(2,1)} %reshape.333), calls=%async_computation.2 | async-start | bytes 131072 | tf_op jit(solution)/shard_map/all_to_all | solution.py:151
  307.8 0.7 add_compare_fusion
  308.6 8.5 %all-to-all-done.2 = bf16[32,2,512]{2,1,0:T(2,128)(2,1)S(1)} async-done(((bf16[32,2,512]{2,1,0:T(2,128)(2,1)}), bf16[32,2,512]{2,1,0:T(2,128)(2,1)S(1)}, u32[]{:S(2)}, u32[]{:S(2)}) %all-to-all-start.2) | async-done | bytes 65568 | tf_op jit(solution)/shard_map/all_to_all | solution.py:151
  317.0 0.1 reshape.334
  317.2 0.1 reshape.263
  317.4 0.2 fusion.99
  317.7 0.9 fusion.58
  318.7 0.6 gather_fusion.1
  319.2 0.4 fusion.100
  319.7 0.6 collective-permute-start.1
  320.3 1.1 collective-permute-start
  321.4 0.4 fusion.15
  321.8 1.3 collective-permute-done.1
  323.0 0.4 fusion.98
  323.4 0.2 fusion.36
  323.6 0.1 collective-permute-done
  323.7 0.4 fusion.13
  324.1 0.2 constant_dynamic-slice_fusion.1
  324.4 0.9 copy.124
  325.3 0.2 fusion.64
  325.5 15.9 %all-gather.1 = f32[64,8,4]{1,2,0:T(4,128)S(1)} all-gather(f32[8,8,4]{1,2,0:T(4,128)S(1)} %fusion.64), channel_id=3, replica_groups=mesh['req'=16,'tp'=8,'pp'=2] {'tp'}, dimensions={0}, use_global_device_ids=true | all-gather | bytes 9216 | tf_op jit(solution)/shard_map/all_gather | solution.py:21
  341.4 12.8 %all-gather = f32[64,8,4]{1,2,0:T(4,128)S(1)} all-gather(f32[8,8,4]{1,2,0:T(4,128)S(1)} %get-tuple-element.103), channel_id=2, replica_groups=mesh['req'=16,'tp'=8,'pp'=2] {'tp'}, dimensions={0}, use_global_device_ids=true | all-gather | bytes 9216 | tf_op jit(solution)/shard_map/all_gather | solution.py:21
  354.2 0.9 slice_bitcast_fusion
  355.2 1.2 slice.94
  356.4 5.4 %while.14 = (s32[]{:T(128)}, f32[1,8,8,4]{2,3,1,0:T(4,128)S(1)}, f32[1,8,8,4]{2,3,1,0:T(4,128)S(1)}, f32[1,8,8,4,128]{4,3,2,1,0:T(4,128)S(1)}, f32[7,1,8,8,4]{3,...) while((s32[]{:T(128)}, f32[1,8,8,4]{2,3,1,0:T(4,128)S(1)}, ...), condition=%wide.region_8.10_spmd, body=%wide.region_7.9_spmd.sunk | while | flops 100098 | bytes 674913 | solution.py:24
  356.8 0.4 fusion.116
  357.6 0.4 fusion.116
  358.3 0.4 fusion.116
  359.1 0.4 fusion.116
  359.9 0.4 fusion.116
  360.6 0.4 fusion.116
  361.4 0.4 fusion.116
  362.0 0.4 fusion.23
  362.4 0.7 convert_element_type.48
  (96 shorter events, 3.5 us)
Async XLA Ops:
  8.0 310.7 %copy-start = (bf16[16,32,512]{2,1,0:T(8,128)(2,1)S(1)}, bf16[16,32,512]{2,1,0:T(8,128)(2,1)}, u32[]{:S(2)}) copy-start(bf16[16,32,512]{2,1,0:T(8,128)(2,1)} %param.23) | copy-start | bytes 1572868
  8.0 158.6 %all-gather.7.cloned.1.call-start = ((), (), s32[]{:S(2)}) async-start(), calls=%async_computation.3 | async-start | bytes 4456448 | tf_op jit(solution)/shard_map/all_gather | solution.py:69
  12.1 12.8 %copy-start.5 = (s32[32]{0:T(128)S(1)}, s32[32]{0:T(128)}, u32[]{:S(2)}) copy-start(s32[32]{0:T(128)} %param.18) | copy-start | bytes 388
  12.1 122.2 %all-to-all-start = ((bf16[16,4,8,4096]{3,2,1,0:T(8,128)(2,1)}), bf16[16,4,8,4096]{3,2,1,0:T(8,128)(2,1)}, u32[]{:S(2)}, u32[]{:S(2)}) async-start(bf16[16,4,8,4096]{3,2,1,0:T(8,128)(2,1)} %stack.8), calls=%async_computation | async-start | bytes 8388608 | tf_op jit(solution)/shard_map/all_to_all | solution.py:75
  24.1 241.6 %all-gather.9.cloned.1.call-start = ((), (), s32[]{:S(2)}) async-start(), calls=%async_computation.4 | async-start | bytes 4456448 | tf_op jit(solution)/shard_map/all_gather | solution.py:70
  24.8 258.0 %all-reduce.4.cloned.1.call-start = ((), (), s32[]{:S(2)}) async-start(), calls=%async_computation.6 | async-start | bytes 2621440 | tf_op jit(solution)/shard_map/psum | solution.py:91
  25.0 112.0 %copy-start.2 = (bf16[4096,64]{0,1:T(8,128)(2,1)S(1)}, bf16[4096,64]{0,1:T(8,128)(2,1)}, u32[]{:S(2)}) copy-start(bf16[4096,64]{0,1:T(8,128)(2,1)} %param.20) | copy-start | bytes 1572868
  137.0 1.4 copy-start.3
  137.0 2.8 copy-start.6
  142.3 2.7 copy-start.8
  272.2 36.3 %copy-start.4 = (bf16[1,4,2,1024]{3,2,1,0:T(2,128)(2,1)S(1)}, bf16[1,4,2,1024]{3,2,1,0:T(2,128)(2,1)}, u32[]{:S(2)}) copy-start(bf16[1,4,2,1024]{3,2,1,0:T(2,128)(2,1)} %param.27) | copy-start | bytes 49156
  272.2 45.2 %copy-start.7 = (bf16[1,4,8192]{2,1,0:T(4,128)(2,1)S(1)}, bf16[1,4,8192]{2,1,0:T(4,128)(2,1)}, u32[]{:S(2)}) copy-start(bf16[1,4,8192]{2,1,0:T(4,128)(2,1)} %param.26) | copy-start | bytes 196612
  282.8 38.6 %copy-start.1 = (f32[4,128,512]{2,1,0:T(8,128)S(1)}, f32[4,128,512]{2,1,0:T(8,128)}, u32[]{:S(2)}) copy-start(f32[4,128,512]{2,1,0:T(8,128)} %get-tuple-element.89) | copy-start | bytes 3145732
  286.1 15.1 %all-to-all-start.1 = ((bf16[8,2,2048]{2,1,0:T(2,128)(2,1)}), bf16[8,2,2048]{2,1,0:T(2,128)(2,1)S(1)}, u32[]{:S(2)}, u32[]{:S(2)}) async-start(bf16[8,2,2048]{2,1,0:T(2,128)(2,1)} %reshape.331), calls=%async_computation.1 | async-start | bytes 131072 | tf_op jit(solution)/shard_map/all_to_all | solution.py:152
  302.1 14.9 %all-to-all-start.2 = ((bf16[32,2,512]{2,1,0:T(2,128)(2,1)}), bf16[32,2,512]{2,1,0:T(2,128)(2,1)S(1)}, u32[]{:S(2)}, u32[]{:S(2)}) async-start(bf16[32,2,512]{2,1,0:T(2,128)(2,1)} %reshape.333), calls=%async_computation.2 | async-start | bytes 131072 | tf_op jit(solution)/shard_map/all_to_all | solution.py:151
  307.7 46.5 %all-gather.11.cloned.1.call-start = ((), (), s32[]{:S(2)}) async-start(), calls=%async_computation.5 | async-start | bytes 1179648 | tf_op jit(solution)/shard_map/all_gather | solution.py:21
  319.7 3.4 collective-permute-start.1
  320.3 3.5 collective-permute-start
Sparse Core Ops, SparseCore 0:
  11.8 154.8 all-gather.6
  169.6 96.0 all-gather.8
Sparse Core Ops, SparseCore 1:
  145.1 56.6 all-reduce.3
  318.7 20.3 all-gather.10
